TPU v7x, 32 devices: a whole 2x2x4 slice. The times are simulated.
32 devices in a mesh: seq: 32 (over z, y, x, core).
Axes of the slice: x: 2, y: 2, z: 4, core: 2. Of those that a mesh axis runs over, the one named last changes fastest.
Arguments:
- queries: bfloat16 [4096, 2048], P('seq'), may hold values from -4.5 to 4.5
- keys: bfloat16 [4096, 512], P('seq'), may hold values from -4.5 to 4.5
- values: bfloat16 [4096, 512], P('seq'), may hold values from -6 to 6
- selected: int32 [32, 4, 32], P('seq'), may hold values from 0 to 127, as said below
Outputs:
- attended: bfloat16 [4096, 2048], P('seq')
Inputs may be any that keep to these rules, and one draw needn't show every extreme that they name: Each row selected[b, g] holds 32 distinct positions.
All inputs are finite; a program needn't handle non-finite values.
Results may differ from a plain program's by a relative error of at most 0.005.
Values may be sent and summed in bfloat16 or wider, within the bound.
A program may use at most 192 MiB of HBM per device.

v0:
```python
import math

import jax
import jax.numpy as jnp
from jax import lax
from jax.sharding import PartitionSpec as P

HD = 128
QH = 16
KVH = 4
PASS = 32
TOK_DEV = 128


very_negative = -1e30


def from_root(value, axis, source):
    kept = jnp.where(lax.axis_index(axis) == source, value, 0).astype(value.dtype)
    return lax.psum(kept, axis)


def update(running, query_set, key_rows, value_rows, visible):
    best, totals, weighted = running
    scores = jnp.einsum("tgjd,sgd->gjst", query_set, key_rows, preferred_element_type=jnp.float32)
    scores = jnp.where(visible, scores * (1.0 / math.sqrt(HD)), very_negative)
    new_best = jnp.maximum(best, jnp.max(scores, axis=-2))
    weights = jnp.where(visible, jnp.exp(scores - new_best[..., None, :]), 0.0)
    rescale = jnp.exp(best - new_best)
    totals = totals * rescale + jnp.sum(weights, axis=-2)
    weighted = weighted * rescale[..., None] + jnp.einsum(
        "gjst,sgd->gjtd",
        weights.astype(jnp.bfloat16),
        value_rows,
        preferred_element_type=jnp.float32,
    )
    return (new_best, totals, weighted)


def passing_step(query_set, running, shard_keys, shard_values, low_source, high_source):
    source = jnp.arange(shard_keys.shape[0], dtype=jnp.int32) // PASS
    visible = (source >= low_source) & (source < high_source)

    def compute(current):
        return update(current, query_set, shard_keys, shard_values, visible[None, None, :, None])

    def unchanged(current):
        return current

    return lax.cond(jnp.any(visible), compute, unchanged, running)


def body(queries, keys, values, selected):
    rank_here = lax.axis_index("seq")
    group_size = QH // KVH
    query_heads = queries.reshape(TOK_DEV, KVH, group_size, HD)
    local_keys = keys.reshape(TOK_DEV, KVH, HD)
    local_values = values.reshape(TOK_DEV, KVH, HD)
    empty_state = (
        jnp.full((KVH, group_size, TOK_DEV), very_negative, jnp.float32),
        jnp.zeros((KVH, group_size, TOK_DEV), jnp.float32),
        jnp.zeros((KVH, group_size, TOK_DEV, HD), jnp.float32),
    )
    position = jnp.arange(TOK_DEV, dtype=jnp.int32)
    causal = (position[:, None] <= position[None, :])[None, None]
    own_state = update(empty_state, query_heads, local_keys, local_values, causal)
    anchor_keys, anchor_values = (
        from_root(local_keys, "seq", 0),
        from_root(local_values, "seq", 0),
    )
    anchor_seen = jnp.broadcast_to(rank_here > 0, (1, 1, TOK_DEV, 1))
    own_state = update(own_state, query_heads, anchor_keys, anchor_values, anchor_seen)
    one_hot = (selected[0][:, :, None] == position[None, None, :]).astype(jnp.bfloat16)
    pass_keys = jnp.einsum(
        "gpt,tgd->pgd", one_hot, local_keys, preferred_element_type=jnp.float32
    ).astype(jnp.bfloat16)
    pass_values = jnp.einsum(
        "gpt,tgd->pgd", one_hot, local_values, preferred_element_type=jnp.float32
    ).astype(jnp.bfloat16)
    final_state = passing_step(
        query_heads,
        own_state,
        lax.all_gather(pass_keys, "seq", axis=0, tiled=True),
        lax.all_gather(pass_values, "seq", axis=0, tiled=True),
        1,
        rank_here,
    )
    mixed = final_state[2] / final_state[1][..., None]
    mixed = jnp.transpose(mixed, (2, 0, 1, 3)).reshape(TOK_DEV, QH * HD)
    return mixed.astype(jnp.bfloat16)


def solution(mesh):
    placed = (P("seq", None), P("seq", None), P("seq", None), P("seq", None, None))
    return jax.shard_map(
        body, mesh=mesh, in_specs=placed, out_specs=P("seq", None), check_vma=False
    )
```

profile of v0, /device:TPU:25, one launch (start us, length us, event | category | flops | bytes accessed | tf_op | source)
XLA Modules:
  0.0 263.5 jit_solution(10888235059076133783)
XLA Ops:
  6.5 0.0 all-reduce.3.cloned.1.call-start
  6.5 1.0 copy.10
  7.6 1.0 copy.16
  8.6 0.1 copy.19
  8.7 0.1 copy.14
  8.9 0.7 broadcast_select_fusion
  9.5 0.7 broadcast_select_fusion.1
  10.2 0.0 all-reduce.3.cloned.1.call-update
  10.2 0.0 all-gather.3.cloned.1.call-start
  10.3 1.5 fusion.22
  11.8 0.0 all-gather.3.cloned.1.call-update
  11.8 0.0 all-gather.5.cloned.1.call-start
  11.9 1.5 fusion.23
  13.4 0.0 all-gather.5.cloned.1.call-update
  13.4 0.6 fusion.45
  14.7 1.3 copy.11
  16.0 0.4 fusion.51
  16.4 120.2 %all-reduce.3.cloned.1.call-done = (bf16[128,4,128]{2,0,1:T(8,128)(2,1)}, bf16[128,4,128]{2,0,1:T(8,128)(2,1)}) async-done(((bf16[128,4,128]{2,0,1:T(8,128)(2,1)}, bf16[128,4,128]{2,0,1:T(8,128)(2,1)}), (bf16[128,4,128]{2,0,1:T(8,128)(2,1)}, bf16[128,4,128]{2,0,1:T(8,128)(2,1)})) %all-reduce.3.cloned.1.call-update) | async-done | bytes 262160 | tf_op jit(solution)/shard_map/psum | solution.py:20
  136.6 1.2 fusion.52
  137.8 0.4 fusion.25
  138.3 0.8 fusion.17
  139.1 1.3 convolution_add_fusion
  140.4 51.7 %all-gather.3.cloned.1.call-done = bf16[1024,4,128]{2,0,1:T(8,128)(2,1)} async-done(((bf16[32,4,128]{2,0,1:T(8,128)(2,1)}), bf16[1024,4,128]{2,0,1:T(8,128)(2,1)}) %all-gather.3.cloned.1.call-update) | async-done | bytes 1048592 | tf_op jit(solution)/shard_map/all_gather | solution.py:83
  192.1 54.3 %all-gather.5.cloned.1.call-done = bf16[1024,4,128]{2,0,1:T(8,128)(2,1)} async-done(((bf16[32,4,128]{2,0,1:T(8,128)(2,1)}), bf16[1024,4,128]{2,0,1:T(8,128)(2,1)}) %all-gather.5.cloned.1.call-update) | async-done | bytes 1048592 | tf_op jit(solution)/shard_map/all_gather | solution.py:84
  246.5 8.5 %conditional.1 = ((f32[4,4,128]{2,1,0:T(4,128)S(1)}, f32[4,4,128,128]{3,2,1,0:T(8,128)S(1)})) conditional(s32[]{:T(128)} %convert_element_type.37, (f32[4,4,128]{2,1,0:T(4,128)S(1)}, f32[4,4,128,128]{3,2,1,0:T(8,128)S(1)}) %tuple.12, (pred[1024]{0:T(1024)(128)(4,1)S(1)}, bf16[1024,4,128]{2,0,1:T(8,128)(2,1)}, bf16[128,4,4,128]{0,3,2,1:T(8,128)(2,1)S(1)}, ...), branch_computations={%region_7.8_spmd, %region_8.11_spmd} | conditional | flops 1101533184 | bytes 34196532 | solution.py:50
  246.5 0.0 copy-start
  246.5 2.8 %bitcast_reduce_fusion = (f32[4,4,128]{2,1,0:T(4,128)S(1)}, f32[4,1024,128,4]{2,1,3,0:T(8,128)S(1)}) fusion(pred[1024]{0:T(1024)(128)(4,1)S(1)} %get-tuple-element.25, bf16[128,4,4,128]{0,3,2,1:T(8,128)(2,1)S(1)} %get-tuple-element.36, bf16[1024,4,128]{2,0,1:T(8,128)(2,1)} %get-tuple-element.26), kind=kOutput, calls=%fused_computation.1 | convolution fusion | flops 543160320 | bytes 9970688 | tf_op jit(solution)/shard_map/cond/branch_1_fun/tgjd,sgd->gjst/dot_general | solution.py:25
  249.3 2.5 fusion.3
  251.8 0.0 copy-done
  251.8 3.2 %fusion.8 = f32[4,4,128,128]{3,2,1,0:T(8,128)S(1)} fusion(f32[4,1024,128,4]{2,1,3,0:T(8,128)S(1)} %get-tuple-element.48, f32[4,4,128]{2,1,0:T(4,128)S(1)} %max.12, pred[1024]{0:T(1024)(128)(4,1)S(1)} %get-tuple-element.25, bf16[1024,4,128]{2,0,1:T(8,128)(2,1)S(1)} %copy-done, f32[4,4,128,128]{3,2,1,0:T(8,128)S(1)} %get-tuple-element.28, ...), kind=kOutput, calls=%fused_computation.10 | convolution fusion | flops 547880960 | bytes 11551744 | tf_op jit(solution)/shard_map/cond/branch_1_fun/gjst,sgd->gjtd/dot_general | solution.py:31
  255.0 0.3 fusion.34
  255.4 0.4 copy.24
  255.8 1.2 convert_element_type.46
  (5 shorter events, 0.1 us)
Async XLA Ops:
  6.5 130.1 %all-reduce.3.cloned.1.call-start = ((), (), s32[]{:S(2)}) async-start(), calls=%async_computation.2 | async-start | bytes 524288 | tf_op jit(solution)/shard_map/psum | solution.py:20
  10.2 181.9 %all-gather.3.cloned.1.call-start = ((), (), s32[]{:S(2)}) async-start(), calls=%async_computation | async-start | bytes 1081344 | tf_op jit(solution)/shard_map/all_gather | solution.py:83
  11.8 234.7 %all-gather.5.cloned.1.call-start = ((), (), s32[]{:S(2)}) async-start(), calls=%async_computation.1 | async-start | bytes 1081344 | tf_op jit(solution)/shard_map/all_gather | solution.py:84
  246.5 5.3 %copy-start = (bf16[1024,4,128]{2,0,1:T(8,128)(2,1)S(1)}, bf16[1024,4,128]{2,0,1:T(8,128)(2,1)}, u32[]{:S(2)}) copy-start(bf16[1024,4,128]{2,0,1:T(8,128)(2,1)} %get-tuple-element.29) | copy-start | bytes 3145732 | tf_op jit(solution)/shard_map/cond
Sparse Core Ops, SparseCore 0:
  13.0 123.5 all-reduce.2
  139.5 52.6 all-gather.2
  195.0 51.4 all-gather.4
where the time goes:
time: 265 us; the launch traced here: 264 us
  waiting for transfers between devices  226 us (85%)
  between operations  13.8 us (5%)
  matrix products  12.7 us (5%)
  other arithmetic  5.3 us (2%)
  local copies, waits for them, and re-layouts  5.22 us (2%)
    psum x1, waiting for transfers between devices, from_root(): return lax.psum(kept, axis)  120 us
    all_gather x1, waiting for transfers between devices, body(): lax.all_gather(pass_values, 'seq', axis=0, tiled=True)  54.3 us
    all_gather x1, waiting for transfers between devices, body(): lax.all_gather(pass_keys, 'seq', axis=0, tiled=True)  51.7 us
  transfers between devices with their start and end apart: 3, of which 3 were waited for; matrix products, arithmetic and copies ran while one was open for 3% of the time, Pallas kernels for 0%

commit v1 on v0

v1 whole, which is shorter than its diff:
```python
import functools
import math

import jax
import jax.numpy as jnp
from jax import lax
from jax.experimental import pallas as pl
from jax.experimental.pallas import tpu as pltpu
from jax.sharding import PartitionSpec as P

HD = 128
QH = 16
KVH = 4
PASS = 32
TOK_DEV = 128
GROUP = QH // KVH
PLANE = 8
LOG2_SCALE = math.log2(math.e) / math.sqrt(HD)
very_negative = -1e30
MESH = pl.DeviceIdType.MESH


def dot_t(a, b):
    return lax.dot_general(a, b, (((1,), (1,)), ((), ())), preferred_element_type=jnp.float32)


def dot(a, b):
    return lax.dot_general(a, b, (((1,), (0,)), ((), ())), preferred_element_type=jnp.float32)


def kernel(n, q_ref, k_ref, v_ref, sel_ref, o_ref, buf, anchor, acc, best, tot,
           packet_recv, anchor_recv, packet_send, anchor_send, z_send, anchor_z_send, scatter_send):
    planes = n // PLANE
    me = lax.axis_index("seq")
    plane = me // PLANE
    r = me % PLANE
    core = r % 2
    x = (r // 2) % 2
    y = r // 4
    near_x = r + 2 - 4 * x
    near_y = r + 4 - 8 * y
    first = near_x * (1 - core) + near_y * core
    second = near_y * (1 - core) + near_x * core
    across = near_x + near_y - r
    to_sib = 1 - 2 * core
    home = plane * PLANE

    barrier = pltpu.get_barrier_semaphore()

    def greet_plane(i, carry):
        pl.semaphore_signal(barrier, inc=1, device_id=(home + (r + i) % PLANE,), device_id_type=MESH)
        return carry

    def greet_line(i, carry):
        pl.semaphore_signal(barrier, inc=1, device_id=(((plane + i) % planes) * PLANE + r,), device_id_type=MESH)
        return carry

    lax.fori_loop(1, PLANE, greet_plane, 0)
    lax.fori_loop(1, planes, greet_line, 0)

    lane = lax.broadcasted_iota(jnp.int32, (PASS, PASS), 1)
    row = lax.broadcasted_iota(jnp.int32, (PASS, PASS), 0)
    token = lax.broadcasted_iota(jnp.int32, (PASS, TOK_DEV), 1).astype(jnp.float32)
    for g in range(KVH):
        sel = sel_ref[0, g:g + 1, :].astype(jnp.float32)
        column = jnp.sum(jnp.where(lane == row, sel, 0.0), axis=1, keepdims=True)
        one_hot = jnp.where(token == column, 1.0, 0.0).astype(jnp.bfloat16)
        cols = slice(g * HD, (g + 1) * HD)
        buf[me, g] = dot(one_hot, k_ref[:, cols]).astype(jnp.bfloat16)
        buf[me, KVH + g] = dot(one_hot, v_ref[:, cols]).astype(jnp.bfloat16)

    pl.semaphore_wait(barrier, PLANE - 1 + planes - 1)

    def remote(ref, send_sem, recv_sem, device):
        return pltpu.make_async_remote_copy(
            src_ref=ref, dst_ref=ref, send_sem=send_sem, recv_sem=recv_sem,
            device_id=(device,), device_id_type=MESH)

    class Stage:
        def __init__(self, piece, recv, send):
            self.piece, self.recv, self.send = piece, recv, send

        def arrived(self, rr):
            remote(self.piece(rr), self.send(0), self.recv(rr), home + first).wait_recv()

        def push(self, rr, target, i):
            remote(self.piece(rr), self.send(i), self.recv(rr), home + target).start()

        def issue(self):
            self.push(r, first, 0)
            self.push(r, second, 1)
            self.push(r, r + to_sib, 2)

        def relay(self):
            self.arrived(first)
            self.push(first, second, 3)
            self.push(first, r + to_sib, 4)
            self.arrived(second)
            self.push(second, r + to_sib, 5)

        def finish(self):
            self.arrived(across)
            self.push(across, r + to_sib, 6)

        def gathered(self):
            for rr in (r, first, second, across):
                self.arrived(rr + to_sib)

        def sent(self):
            for i in range(7):
                remote(self.piece(r), self.send(i), self.recv(r), home + first).wait_send()

    def packet(q):
        return Stage(lambda rr: buf.at[q * PLANE + rr], lambda rr: packet_recv.at[q * PLANE + rr],
                     lambda i: packet_send.at[q, i])

    block0 = Stage(lambda rr: anchor.at[rr], lambda rr: anchor_recv.at[rr], lambda i: anchor_send.at[i])

    def send_line(ref, sems, recv_sem):
        def one(other, carry):
            remote(ref, sems.at[other], recv_sem, other * PLANE + r).start()
            return carry

        lax.fori_loop(plane + 1, planes, one, 0)

    def sent_line(ref, sems, recv_sem):
        def one(other, carry):
            remote(ref, sems.at[other], recv_sem, other * PLANE + r).wait_send()
            return carry

        lax.fori_loop(plane + 1, planes, one, 0)

    def scatter(j):
        source = k_ref if j < KVH else v_ref
        cols = pl.ds((j % KVH) * HD, HD)
        return pltpu.make_async_remote_copy(
            src_ref=source.at[:, cols], dst_ref=anchor.at[j], send_sem=scatter_send.at[j],
            recv_sem=anchor_recv.at[j], device_id=(j,), device_id_type=MESH)

    @pl.when(me == 0)
    def _():
        for j in range(1, PLANE):
            scatter(j).start()
        anchor[0] = k_ref[:, :HD]

    send_line(buf.at[me], z_send, packet_recv.at[me])
    packet(plane).issue()

    def head_queries(g):
        return jnp.concatenate(
            [q_ref[:, pl.ds(pl.multiple_of((g * GROUP + j) * HD, HD), HD)] for j in range(GROUP)], axis=0)

    def lane_tiles(w):
        return [w[:, i * HD:(i + 1) * HD] for i in range(w.shape[1] // HD)]

    rows = GROUP * TOK_DEV

    def own(g, carry):
        cols = pl.ds(pl.multiple_of(g * HD, HD), HD)
        s = dot_t(head_queries(g), k_ref[:, cols]) * LOG2_SCALE
        position = lax.broadcasted_iota(jnp.int32, (rows, TOK_DEV), 0) % TOK_DEV
        key_at = lax.broadcasted_iota(jnp.int32, (rows, TOK_DEV), 1)
        s = jnp.where(key_at <= position, s, very_negative)
        top = jnp.broadcast_to(jnp.max(s, axis=1, keepdims=True), (rows, HD))
        w = jnp.exp2(s - top)
        best[g] = top
        tot[g] = w
        acc[g] = dot(w.astype(jnp.bfloat16), v_ref[:, cols])
        return carry

    def update(g, key_rows, value_rows, bias):
        s = dot_t(head_queries(g), key_rows) * LOG2_SCALE
        if bias is not None:
            s = s + bias
        tiles = lane_tiles(s)
        old = best[g]
        top = jnp.max(functools.reduce(jnp.maximum, tiles), axis=1, keepdims=True)
        top = jnp.maximum(old, top)
        w = [jnp.exp2(t - top) for t in tiles]
        rescale = jnp.exp2(old - top)
        best[g] = top
        tot[g] = tot[g] * rescale + functools.reduce(jnp.add, w)
        w = jnp.concatenate([t.astype(jnp.bfloat16) for t in w], axis=1)
        acc[g] = acc[g] * rescale + dot(w, value_rows)

    def use_packets(q):
        source = q * PLANE + lax.broadcasted_iota(jnp.int32, (1, PLANE * PASS), 1) // PASS
        bias = jnp.where((source >= 1) & (source < me), 0.0, very_negative)
        at = pl.ds(q * PLANE, PLANE)

        def one(g, carry):
            update(g, buf[at, g].reshape(PLANE * PASS, HD), buf[at, KVH + g].reshape(PLANE * PASS, HD), bias)
            return carry

        lax.fori_loop(0, KVH, one, 0)

    def use_anchor():
        def one(g, carry):
            update(g, anchor[g], anchor[KVH + g], None)
            return carry

        lax.fori_loop(0, KVH, one, 0)

    lax.fori_loop(0, KVH, own, 0)

    last = plane + 1

    def step(t, carry):
        def at_stage(s, packets, block):
            @pl.when((s >= 0) & (s <= plane))
            def _():
                packets(plane - s)

            @pl.when(s == last)
            def _():
                block()

        def issue_packets(q):
            packet(q).arrived(r)
            packet(q).issue()

        def issue_block():
            @pl.when(me > 0)
            def _():
                block0.arrived(r)

            send_line(anchor.at[r], anchor_z_send, anchor_recv.at[r])
            block0.issue()

        def issue_block_later():
            block0.arrived(r)
            block0.issue()

        def issue_any():
            @pl.when(plane == 0)
            def _():
                issue_block()

            @pl.when(plane > 0)
            def _():
                issue_block_later()

        def compute_packets(q):
            packet(q).gathered()
            use_packets(q)

        def compute_block():
            block0.gathered()

            @pl.when(me > 0)
            def _():
                use_anchor()

        at_stage(t, issue_packets, issue_any)
        at_stage(t - 1, lambda q: packet(q).relay(), block0.relay)
        at_stage(t - 2, lambda q: packet(q).finish(), block0.finish)
        at_stage(t - 3, compute_packets, compute_block)
        return carry

    lax.fori_loop(1, last + 4, step, 0)

    for g in range(KVH):
        out = acc[g] / jnp.sum(tot[g], axis=1, keepdims=True)
        for j in range(GROUP):
            h = g * GROUP + j
            o_ref[:, h * HD:(h + 1) * HD] = out[j * TOK_DEV:(j + 1) * TOK_DEV].astype(o_ref.dtype)

    def drain(q, carry):
        packet(q).sent()
        return carry

    lax.fori_loop(0, plane + 1, drain, 0)
    block0.sent()
    sent_line(buf.at[me], z_send, packet_recv.at[me])

    @pl.when(plane == 0)
    def _():
        sent_line(anchor.at[r], anchor_z_send, anchor_recv.at[r])

    @pl.when(me == 0)
    def _():
        for j in range(1, PLANE):
            scatter(j).wait_send()


def body(n, queries, keys, values, selected):
    planes = n // PLANE
    rows = GROUP * TOK_DEV
    vmem = pl.BlockSpec(memory_space=pltpu.VMEM)
    return pl.pallas_call(
        functools.partial(kernel, n),
        out_shape=jax.ShapeDtypeStruct((TOK_DEV, QH * HD), jnp.bfloat16),
        in_specs=[vmem] * 4,
        out_specs=vmem,
        scratch_shapes=[
            pltpu.VMEM((n, 2 * KVH, PASS, HD), jnp.bfloat16),
            pltpu.VMEM((PLANE, TOK_DEV, HD), jnp.bfloat16),
            pltpu.VMEM((KVH, rows, HD), jnp.float32),
            pltpu.VMEM((KVH, rows, HD), jnp.float32),
            pltpu.VMEM((KVH, rows, HD), jnp.float32),
            pltpu.SemaphoreType.DMA((n,)),
            pltpu.SemaphoreType.DMA((PLANE,)),
            pltpu.SemaphoreType.DMA((planes, 7)),
            pltpu.SemaphoreType.DMA((7,)),
            pltpu.SemaphoreType.DMA((planes,)),
            pltpu.SemaphoreType.DMA((planes,)),
            pltpu.SemaphoreType.DMA((PLANE,)),
        ],
        compiler_params=pltpu.CompilerParams(
            collective_id=0, has_side_effects=True, vmem_limit_bytes=48 * 1024 * 1024),
        cost_estimate=pl.CostEstimate(flops=1300000000, bytes_accessed=4000000, transcendentals=2500000),
    )(queries, keys, values, selected)


def solution(mesh):
    placed = (P("seq", None), P("seq", None), P("seq", None), P("seq", None, None))
    return jax.shard_map(
        functools.partial(body, mesh.shape["seq"]), mesh=mesh, in_specs=placed,
        out_specs=P("seq", None), check_vma=False)
```

time: 265 us -> 32 us (0.12)
  the two profiles are of different devices: /device:TPU:25 before, /device:TPU:24 now
where the time goes in v1:
time: 32 us; the launch traced here: 31.8 us
  Pallas kernels  27.4 us (86%)
  local copies, waits for them, and re-layouts  4.33 us (14%)
    pallas_call x1, Pallas kernels, body(): pl.pallas_call(functools.partial(kernel, n), out_shape=jax.ShapeDtypeStru...  27.4 us
    unnamed x9, local copies, waits for them, and re-layouts  4.33 us

profile of v1, /device:TPU:24, one launch (start us, length us, event | category | flops | bytes accessed | tf_op | source)
XLA Modules:
  0.0 31.8 jit_solution(5302076293299319303)
XLA Ops:
  0.0 0.0 copy-start
  0.0 1.0 %copy-done = bf16[128,2048]{1,0:T(8,128)(2,1)S(1)} copy-done((bf16[128,2048]{1,0:T(8,128)(2,1)S(1)}, bf16[128,2048]{1,0:T(8,128)(2,1)}, u32[]{:S(2)}) %copy-start) | copy-done | bytes 524312
  1.0 0.0 copy-start.1
  1.0 0.9 %copy-done.1 = bf16[128,512]{1,0:T(8,128)(2,1)S(1)} copy-done((bf16[128,512]{1,0:T(8,128)(2,1)S(1)}, bf16[128,512]{1,0:T(8,128)(2,1)}, u32[]{:S(2)}) %copy-start.1) | copy-done | bytes 131096
  1.9 0.0 copy-start.2
  1.9 0.9 %copy-done.2 = bf16[128,512]{1,0:T(8,128)(2,1)S(1)} copy-done((bf16[128,512]{1,0:T(8,128)(2,1)S(1)}, bf16[128,512]{1,0:T(8,128)(2,1)}, u32[]{:S(2)}) %copy-start.2) | copy-done | bytes 131096
  2.9 0.0 copy-start.3
  2.9 0.7 %copy-done.3 = s32[1,4,32]{2,1,0:T(4,128)S(1)} copy-done((s32[1,4,32]{2,1,0:T(4,128)S(1)}, s32[1,4,32]{2,1,0:T(4,128)}, u32[]{:S(2)}) %copy-start.3) | copy-done | bytes 536
  3.5 27.4 %shard_map.46 = bf16[128,2048]{1,0:T(8,128)(2,1)S(1)} custom-call(bf16[128,2048]{1,0:T(8,128)(2,1)S(1)} %copy-done, bf16[128,512]{1,0:T(8,128)(2,1)S(1)} %copy-done.1, bf16[128,512]{1,0:T(8,128)(2,1)S(1)} %copy-done.2, s32[1,4,32]{2,1,0:T(4,128)S(1)} %copy-done.3), custom_call_target="tpu_custom_call" | custom-call | flops 1300000000 | bytes 4000000 | tf_op jit(solution)/shard_map/pallas_call | solution.py:290
  31.0 0.8 %copy.6 = bf16[128,2048]{1,0:T(8,128)(2,1)} copy(bf16[128,2048]{1,0:T(8,128)(2,1)S(1)} %shard_map.46) | data formatting | bytes 1048576
Async XLA Ops:
  0.0 1.0 %copy-start = (bf16[128,2048]{1,0:T(8,128)(2,1)S(1)}, bf16[128,2048]{1,0:T(8,128)(2,1)}, u32[]{:S(2)}) copy-start(bf16[128,2048]{1,0:T(8,128)(2,1)} %q_ref.1) | copy-start | bytes 1572868
  1.0 0.9 %copy-start.1 = (bf16[128,512]{1,0:T(8,128)(2,1)S(1)}, bf16[128,512]{1,0:T(8,128)(2,1)}, u32[]{:S(2)}) copy-start(bf16[128,512]{1,0:T(8,128)(2,1)} %k_ref.1) | copy-start | bytes 393220
  1.9 0.9 %copy-start.2 = (bf16[128,512]{1,0:T(8,128)(2,1)S(1)}, bf16[128,512]{1,0:T(8,128)(2,1)}, u32[]{:S(2)}) copy-start(bf16[128,512]{1,0:T(8,128)(2,1)} %v_ref.1) | copy-start | bytes 393220
  2.9 0.7 %copy-start.3 = (s32[1,4,32]{2,1,0:T(4,128)S(1)}, s32[1,4,32]{2,1,0:T(4,128)}, u32[]{:S(2)}) copy-start(s32[1,4,32]{2,1,0:T(4,128)} %sel_ref.1) | copy-start | bytes 1540

commit v2 on v1

--- a/solution.py
+++ b/solution.py
@@ -28,8 +28,8 @@
     return lax.dot_general(a, b, (((1,), (0,)), ((), ())), preferred_element_type=jnp.float32)
 
 
-def kernel(n, q_ref, k_ref, v_ref, sel_ref, o_ref, buf, anchor, acc, best, tot,
-           packet_recv, anchor_recv, packet_send, anchor_send, z_send, anchor_z_send, scatter_send):
+def kernel(n, q_hbm, k_hbm, v_hbm, sel_hbm, o_ref, q_ref, k_ref, v_ref, sel_ref, buf, anchor, acc, best, tot,
+           packet_recv, anchor_recv, packet_send, anchor_send, scatter_send, load_sem):
     planes = n // PLANE
     me = lax.axis_index("seq")
     plane = me // PLANE
@@ -47,16 +47,38 @@
 
     barrier = pltpu.get_barrier_semaphore()
 
-    def greet_plane(i, carry):
-        pl.semaphore_signal(barrier, inc=1, device_id=(home + (r + i) % PLANE,), device_id_type=MESH)
-        return carry
-
-    def greet_line(i, carry):
-        pl.semaphore_signal(barrier, inc=1, device_id=(((plane + i) % planes) * PLANE + r,), device_id_type=MESH)
-        return carry
-
-    lax.fori_loop(1, PLANE, greet_plane, 0)
-    lax.fori_loop(1, planes, greet_line, 0)
+    loads = [pltpu.make_async_copy(src, dst, load_sem.at[i]) for i, (src, dst) in enumerate(
+        ((sel_hbm, sel_ref), (k_hbm, k_ref), (v_hbm, v_ref), (q_hbm, q_ref)))]
+    for load in loads:
+        load.start()
+
+    def greet(device):
+        pl.semaphore_signal(barrier, inc=1, device_id=(device,), device_id_type=MESH)
+
+    for near in (near_x, near_y, r + to_sib):
+        greet(home + near)
+
+    @pl.when(plane > 0)
+    def _():
+        greet(me - PLANE)
+
+    @pl.when(plane < planes - 1)
+    def _():
+        greet(me + PLANE)
+
+    is_far = (plane == 0) & (core + x + y >= 2)
+
+    @pl.when(me == 0)
+    def _():
+        for far in (3, 5, 6, 7):
+            greet(far)
+
+    @pl.when(is_far)
+    def _():
+        greet(0)
+
+    for load in loads[:3]:
+        load.wait()
 
     lane = lax.broadcasted_iota(jnp.int32, (PASS, PASS), 1)
     row = lax.broadcasted_iota(jnp.int32, (PASS, PASS), 0)
@@ -69,7 +91,9 @@
         buf[me, g] = dot(one_hot, k_ref[:, cols]).astype(jnp.bfloat16)
         buf[me, KVH + g] = dot(one_hot, v_ref[:, cols]).astype(jnp.bfloat16)
 
-    pl.semaphore_wait(barrier, PLANE - 1 + planes - 1)
+    peers = (3 + jnp.where(plane > 0, 1, 0) + jnp.where(plane < planes - 1, 1, 0)
+             + jnp.where(me == 0, 4, 0) + jnp.where(is_far, 1, 0))
+    pl.semaphore_wait(barrier, peers)
 
     def remote(ref, send_sem, recv_sem, device):
         return pltpu.make_async_remote_copy(
@@ -87,6 +111,10 @@
             remote(self.piece(rr), self.send(i), self.recv(rr), home + target).start()
 
         def issue(self):
+            @pl.when(plane < planes - 1)
+            def _():
+                remote(self.piece(r), self.send(7), self.recv(r), me + PLANE).start()
+
             self.push(r, first, 0)
             self.push(r, second, 1)
             self.push(r, r + to_sib, 2)
@@ -110,25 +138,15 @@
             for i in range(7):
                 remote(self.piece(r), self.send(i), self.recv(r), home + first).wait_send()
 
+            @pl.when(plane < planes - 1)
+            def _():
+                remote(self.piece(r), self.send(7), self.recv(r), me + PLANE).wait_send()
+
     def packet(q):
         return Stage(lambda rr: buf.at[q * PLANE + rr], lambda rr: packet_recv.at[q * PLANE + rr],
                      lambda i: packet_send.at[q, i])
 
     block0 = Stage(lambda rr: anchor.at[rr], lambda rr: anchor_recv.at[rr], lambda i: anchor_send.at[i])
-
-    def send_line(ref, sems, recv_sem):
-        def one(other, carry):
-            remote(ref, sems.at[other], recv_sem, other * PLANE + r).start()
-            return carry
-
-        lax.fori_loop(plane + 1, planes, one, 0)
-
-    def sent_line(ref, sems, recv_sem):
-        def one(other, carry):
-            remote(ref, sems.at[other], recv_sem, other * PLANE + r).wait_send()
-            return carry
-
-        lax.fori_loop(plane + 1, planes, one, 0)
 
     def scatter(j):
         source = k_ref if j < KVH else v_ref
@@ -143,7 +161,6 @@
             scatter(j).start()
         anchor[0] = k_ref[:, :HD]
 
-    send_line(buf.at[me], z_send, packet_recv.at[me])
     packet(plane).issue()
 
     def head_queries(g):
@@ -201,6 +218,7 @@
 
         lax.fori_loop(0, KVH, one, 0)
 
+    loads[3].wait()
     lax.fori_loop(0, KVH, own, 0)
 
     last = plane + 1
@@ -224,21 +242,7 @@
             def _():
                 block0.arrived(r)
 
-            send_line(anchor.at[r], anchor_z_send, anchor_recv.at[r])
             block0.issue()
-
-        def issue_block_later():
-            block0.arrived(r)
-            block0.issue()
-
-        def issue_any():
-            @pl.when(plane == 0)
-            def _():
-                issue_block()
-
-            @pl.when(plane > 0)
-            def _():
-                issue_block_later()
 
         def compute_packets(q):
             packet(q).gathered()
@@ -251,7 +255,7 @@
             def _():
                 use_anchor()
 
-        at_stage(t, issue_packets, issue_any)
+        at_stage(t, issue_packets, issue_block)
         at_stage(t - 1, lambda q: packet(q).relay(), block0.relay)
         at_stage(t - 2, lambda q: packet(q).finish(), block0.finish)
         at_stage(t - 3, compute_packets, compute_block)
@@ -271,11 +275,6 @@
 
     lax.fori_loop(0, plane + 1, drain, 0)
     block0.sent()
-    sent_line(buf.at[me], z_send, packet_recv.at[me])
-
-    @pl.when(plane == 0)
-    def _():
-        sent_line(anchor.at[r], anchor_z_send, anchor_recv.at[r])
 
     @pl.when(me == 0)
     def _():
@@ -290,9 +289,13 @@
     return pl.pallas_call(
         functools.partial(kernel, n),
         out_shape=jax.ShapeDtypeStruct((TOK_DEV, QH * HD), jnp.bfloat16),
-        in_specs=[vmem] * 4,
+        in_specs=[pl.BlockSpec(memory_space=pltpu.HBM)] * 4,
         out_specs=vmem,
         scratch_shapes=[
+            pltpu.VMEM(queries.shape, queries.dtype),
+            pltpu.VMEM(keys.shape, keys.dtype),
+            pltpu.VMEM(values.shape, values.dtype),
+            pltpu.VMEM(selected.shape, selected.dtype),
             pltpu.VMEM((n, 2 * KVH, PASS, HD), jnp.bfloat16),
             pltpu.VMEM((PLANE, TOK_DEV, HD), jnp.bfloat16),
             pltpu.VMEM((KVH, rows, HD), jnp.float32),
@@ -300,11 +303,10 @@
             pltpu.VMEM((KVH, rows, HD), jnp.float32),
             pltpu.SemaphoreType.DMA((n,)),
             pltpu.SemaphoreType.DMA((PLANE,)),
-            pltpu.SemaphoreType.DMA((planes, 7)),
-            pltpu.SemaphoreType.DMA((7,)),
-            pltpu.SemaphoreType.DMA((planes,)),
-            pltpu.SemaphoreType.DMA((planes,)),
+            pltpu.SemaphoreType.DMA((planes, 8)),
+            pltpu.SemaphoreType.DMA((8,)),
             pltpu.SemaphoreType.DMA((PLANE,)),
+            pltpu.SemaphoreType.DMA((4,)),
         ],
         compiler_params=pltpu.CompilerParams(
             collective_id=0, has_side_effects=True, vmem_limit_bytes=48 * 1024 * 1024),

time: 32 us -> 30.3 us (0.947)
  Pallas kernels: 27.4 us -> 25.7 us
    pallas_call x1, Pallas kernels: 27.4 us -> 25.7 us  [body(): pl.pallas_call(functools.partial(kernel, n), out_shape=jax.ShapeDtypeStru...]
where the time goes in v2:
time: 30.3 us; the launch traced here: 30.1 us
  Pallas kernels  25.7 us (85%)
  local copies, waits for them, and re-layouts  4.33 us (14%)
    pallas_call x1, Pallas kernels, body(): pl.pallas_call(functools.partial(kernel, n), out_shape=jax.ShapeDtypeStru...  25.7 us
    unnamed x9, local copies, waits for them, and re-layouts  4.33 us

profile of v2, /device:TPU:24, one launch (start us, length us, event | category | flops | bytes accessed | tf_op | source)
XLA Modules:
  0.0 30.1 jit_solution(11247290765681767168)
XLA Ops:
  0.0 0.0 copy-start
  0.0 1.0 %copy-done = bf16[128,2048]{1,0:T(8,128)(2,1)S(1)} copy-done((bf16[128,2048]{1,0:T(8,128)(2,1)S(1)}, bf16[128,2048]{1,0:T(8,128)(2,1)}, u32[]{:S(2)}) %copy-start) | copy-done | bytes 524312
  1.0 0.0 copy-start.1
  1.0 0.9 %copy-done.1 = bf16[128,512]{1,0:T(8,128)(2,1)S(1)} copy-done((bf16[128,512]{1,0:T(8,128)(2,1)S(1)}, bf16[128,512]{1,0:T(8,128)(2,1)}, u32[]{:S(2)}) %copy-start.1) | copy-done | bytes 131096
  1.9 0.0 copy-start.2
  1.9 0.9 %copy-done.2 = bf16[128,512]{1,0:T(8,128)(2,1)S(1)} copy-done((bf16[128,512]{1,0:T(8,128)(2,1)S(1)}, bf16[128,512]{1,0:T(8,128)(2,1)}, u32[]{:S(2)}) %copy-start.2) | copy-done | bytes 131096
  2.9 0.0 copy-start.3
  2.9 0.7 %copy-done.3 = s32[1,4,32]{2,1,0:T(4,128)S(1)} copy-done((s32[1,4,32]{2,1,0:T(4,128)S(1)}, s32[1,4,32]{2,1,0:T(4,128)}, u32[]{:S(2)}) %copy-start.3) | copy-done | bytes 536
  3.5 25.7 %shard_map.46 = bf16[128,2048]{1,0:T(8,128)(2,1)S(1)} custom-call(bf16[128,2048]{1,0:T(8,128)(2,1)S(1)} %copy-done, bf16[128,512]{1,0:T(8,128)(2,1)S(1)} %copy-done.1, bf16[128,512]{1,0:T(8,128)(2,1)S(1)} %copy-done.2, s32[1,4,32]{2,1,0:T(4,128)S(1)} %copy-done.3), custom_call_target="tpu_custom_call" | custom-call | flops 1300000000 | bytes 4000000 | tf_op jit(solution)/shard_map/pallas_call | solution.py:289
  29.3 0.8 %copy.6 = bf16[128,2048]{1,0:T(8,128)(2,1)} copy(bf16[128,2048]{1,0:T(8,128)(2,1)S(1)} %shard_map.46) | data formatting | bytes 1048576
Async XLA Ops:
  0.0 1.0 %copy-start = (bf16[128,2048]{1,0:T(8,128)(2,1)S(1)}, bf16[128,2048]{1,0:T(8,128)(2,1)}, u32[]{:S(2)}) copy-start(bf16[128,2048]{1,0:T(8,128)(2,1)} %q_hbm.1) | copy-start | bytes 1572868
  1.0 0.9 %copy-start.1 = (bf16[128,512]{1,0:T(8,128)(2,1)S(1)}, bf16[128,512]{1,0:T(8,128)(2,1)}, u32[]{:S(2)}) copy-start(bf16[128,512]{1,0:T(8,128)(2,1)} %k_hbm.1) | copy-start | bytes 393220
  1.9 0.9 %copy-start.2 = (bf16[128,512]{1,0:T(8,128)(2,1)S(1)}, bf16[128,512]{1,0:T(8,128)(2,1)}, u32[]{:S(2)}) copy-start(bf16[128,512]{1,0:T(8,128)(2,1)} %v_hbm.1) | copy-start | bytes 393220
  2.9 0.7 %copy-start.3 = (s32[1,4,32]{2,1,0:T(4,128)S(1)}, s32[1,4,32]{2,1,0:T(4,128)}, u32[]{:S(2)}) copy-start(s32[1,4,32]{2,1,0:T(4,128)} %sel_hbm.1) | copy-start | bytes 1540

commit v3 on v2

--- a/solution.py
+++ b/solution.py
@@ -209,17 +209,17 @@
             update(g, buf[at, g].reshape(PLANE * PASS, HD), buf[at, KVH + g].reshape(PLANE * PASS, HD), bias)
             return carry
 
-        lax.fori_loop(0, KVH, one, 0)
+        lax.fori_loop(0, KVH, one, 0, unroll=True)
 
     def use_anchor():
         def one(g, carry):
             update(g, anchor[g], anchor[KVH + g], None)
             return carry
 
-        lax.fori_loop(0, KVH, one, 0)
+        lax.fori_loop(0, KVH, one, 0, unroll=True)
 
     loads[3].wait()
-    lax.fori_loop(0, KVH, own, 0)
+    lax.fori_loop(0, KVH, own, 0, unroll=True)
 
     last = plane + 1
 
@@ -309,7 +309,7 @@
             pltpu.SemaphoreType.DMA((4,)),
         ],
         compiler_params=pltpu.CompilerParams(
-            collective_id=0, has_side_effects=True, vmem_limit_bytes=48 * 1024 * 1024),
+            collective_id=0, has_side_effects=True, vmem_limit_bytes=60 * 1024 * 1024),
         cost_estimate=pl.CostEstimate(flops=1300000000, bytes_accessed=4000000, transcendentals=2500000),
     )(queries, keys, values, selected)
 

time: 30.3 us -> 26.5 us (0.87)
  the two profiles are of different devices: /device:TPU:24 before, /device:TPU:25 now
where the time goes in v3:
time: 26.5 us; the launch traced here: 26.3 us
  Pallas kernels  24.4 us (92%)
  local copies, waits for them, and re-layouts  1.88 us (7%)
    pallas_call x1, Pallas kernels, body(): pl.pallas_call(functools.partial(kernel, n), out_shape=jax.ShapeDtypeStru...  24.4 us
    unnamed x1, local copies, waits for them, and re-layouts  1.88 us

profile of v3, /device:TPU:25, one launch (start us, length us, event | category | flops | bytes accessed | tf_op | source)
XLA Modules:
  0.0 26.3 jit_solution(9936896065887801693)
XLA Ops:
  0.0 24.4 %shard_map.46 = bf16[128,2048]{1,0:T(8,128)(2,1)} custom-call(bf16[128,2048]{1,0:T(8,128)(2,1)} %q_hbm.1, bf16[128,512]{1,0:T(8,128)(2,1)} %k_hbm.1, bf16[128,512]{1,0:T(8,128)(2,1)} %v_hbm.1, s32[1,4,32]{2,1,0:T(4,128)} %sel_hbm.1), custom_call_target="tpu_custom_call" | custom-call | flops 1300000000 | bytes 4000000 | tf_op jit(solution)/shard_map/pallas_call | solution.py:289
  24.4 1.9 %copy.6 = bf16[128,2048]{1,0:T(8,128)(2,1)} copy(bf16[128,2048]{1,0:T(8,128)(2,1)} %shard_map.46) | data formatting | bytes 1048576

commit v4 on v3

--- a/solution.py
+++ b/solution.py
@@ -257,8 +257,8 @@
 
         at_stage(t, issue_packets, issue_block)
         at_stage(t - 1, lambda q: packet(q).relay(), block0.relay)
+        at_stage(t - 3, compute_packets, compute_block)
         at_stage(t - 2, lambda q: packet(q).finish(), block0.finish)
-        at_stage(t - 3, compute_packets, compute_block)
         return carry
 
     lax.fori_loop(1, last + 4, step, 0)

time: 26.5 us -> 26.5 us (level)
  no operation moved by 1% of the time
where the time goes in v4:
time: 26.5 us; the launch traced here: 26.3 us
  Pallas kernels  24.4 us (92%)
  local copies, waits for them, and re-layouts  1.88 us (7%)
    pallas_call x1, Pallas kernels, body(): pl.pallas_call(functools.partial(kernel, n), out_shape=jax.ShapeDtypeStru...  24.4 us
    unnamed x1, local copies, waits for them, and re-layouts  1.88 us

profile of v4, /device:TPU:25, one launch (start us, length us, event | category | flops | bytes accessed | tf_op | source)
XLA Modules:
  0.0 26.3 jit_solution(1997664119573215096)
XLA Ops:
  0.0 24.4 %shard_map.46 = bf16[128,2048]{1,0:T(8,128)(2,1)} custom-call(bf16[128,2048]{1,0:T(8,128)(2,1)} %q_hbm.1, bf16[128,512]{1,0:T(8,128)(2,1)} %k_hbm.1, bf16[128,512]{1,0:T(8,128)(2,1)} %v_hbm.1, s32[1,4,32]{2,1,0:T(4,128)} %sel_hbm.1), custom_call_target="tpu_custom_call" | custom-call | flops 1300000000 | bytes 4000000 | tf_op jit(solution)/shard_map/pallas_call | solution.py:289
  24.5 1.9 %copy.6 = bf16[128,2048]{1,0:T(8,128)(2,1)} copy(bf16[128,2048]{1,0:T(8,128)(2,1)} %shard_map.46) | data formatting | bytes 1048576

commit v5 on v4

--- a/solution.py
+++ b/solution.py
@@ -211,12 +211,9 @@
 
         lax.fori_loop(0, KVH, one, 0, unroll=True)
 
-    def use_anchor():
-        def one(g, carry):
-            update(g, anchor[g], anchor[KVH + g], None)
-            return carry
-
-        lax.fori_loop(0, KVH, one, 0, unroll=True)
+    def use_anchor(head):
+        for i in range(2):
+            update(head + i, anchor[head + i], anchor[KVH + head + i], None)
 
     loads[3].wait()
     lax.fori_loop(0, KVH, own, 0, unroll=True)
@@ -249,11 +246,13 @@
             use_packets(q)
 
         def compute_block():
-            block0.gathered()
-
-            @pl.when(me > 0)
-            def _():
-                use_anchor()
+            for rr, other, column in ((r, near_y, x), (near_x, across, 1 - x)):
+                block0.arrived(rr + to_sib)
+                block0.arrived(other + to_sib)
+
+                @pl.when(me > 0)
+                def _():
+                    use_anchor(2 * column)
 
         at_stage(t, issue_packets, issue_block)
         at_stage(t - 1, lambda q: packet(q).relay(), block0.relay)

time: 26.5 us -> 26.3 us (level)
  no operation moved by 1% of the time
where the time goes in v5:
time: 26.3 us; the launch traced here: 26.2 us
  Pallas kernels  24.3 us (92%)
  local copies, waits for them, and re-layouts  1.88 us (7%)
    pallas_call x1, Pallas kernels, body(): pl.pallas_call(functools.partial(kernel, n), out_shape=jax.ShapeDtypeStru...  24.3 us
    unnamed x1, local copies, waits for them, and re-layouts  1.88 us

profile of v5, /device:TPU:25, one launch (start us, length us, event | category | flops | bytes accessed | tf_op | source)
XLA Modules:
  0.0 26.2 jit_solution(4570740860045816026)
XLA Ops:
  0.0 24.3 %shard_map.46 = bf16[128,2048]{1,0:T(8,128)(2,1)} custom-call(bf16[128,2048]{1,0:T(8,128)(2,1)} %q_hbm.1, bf16[128,512]{1,0:T(8,128)(2,1)} %k_hbm.1, bf16[128,512]{1,0:T(8,128)(2,1)} %v_hbm.1, s32[1,4,32]{2,1,0:T(4,128)} %sel_hbm.1), custom_call_target="tpu_custom_call" | custom-call | flops 1300000000 | bytes 4000000 | tf_op jit(solution)/shard_map/pallas_call | solution.py:288
  24.3 1.9 %copy.6 = bf16[128,2048]{1,0:T(8,128)(2,1)} copy(bf16[128,2048]{1,0:T(8,128)(2,1)} %shard_map.46) | data formatting | bytes 1048576

commit v6 on v5

--- a/solution.py
+++ b/solution.py
@@ -263,7 +263,7 @@
     lax.fori_loop(1, last + 4, step, 0)
 
     for g in range(KVH):
-        out = acc[g] / jnp.sum(tot[g], axis=1, keepdims=True)
+        out = acc[g] * (1.0 / jnp.sum(tot[g], axis=1, keepdims=True))
         for j in range(GROUP):
             h = g * GROUP + j
             o_ref[:, h * HD:(h + 1) * HD] = out[j * TOK_DEV:(j + 1) * TOK_DEV].astype(o_ref.dtype)

time: 26.3 us -> 26.3 us (level)
  no operation moved by 1% of the time
where the time goes in v6:
time: 26.3 us; the launch traced here: 26.2 us
  Pallas kernels  24.3 us (92%)
  local copies, waits for them, and re-layouts  1.88 us (7%)
    pallas_call x1, Pallas kernels, body(): pl.pallas_call(functools.partial(kernel, n), out_shape=jax.ShapeDtypeStru...  24.3 us
    unnamed x1, local copies, waits for them, and re-layouts  1.88 us

profile of v6, /device:TPU:25, one launch (start us, length us, event | category | flops | bytes accessed | tf_op | source)
XLA Modules:
  0.0 26.2 jit_solution(4570740860045816026)
XLA Ops:
  0.0 24.3 %shard_map.46 = bf16[128,2048]{1,0:T(8,128)(2,1)} custom-call(bf16[128,2048]{1,0:T(8,128)(2,1)} %q_hbm.1, bf16[128,512]{1,0:T(8,128)(2,1)} %k_hbm.1, bf16[128,512]{1,0:T(8,128)(2,1)} %v_hbm.1, s32[1,4,32]{2,1,0:T(4,128)} %sel_hbm.1), custom_call_target="tpu_custom_call" | custom-call | flops 1300000000 | bytes 4000000 | tf_op jit(solution)/shard_map/pallas_call | solution.py:288
  24.3 1.9 %copy.6 = bf16[128,2048]{1,0:T(8,128)(2,1)} copy(bf16[128,2048]{1,0:T(8,128)(2,1)} %shard_map.46) | data formatting | bytes 1048576
